TPU v7x, 32 devices: a whole 2x2x4 slice. The times are simulated.
32 devices in a mesh: mob: 2 (over x), imm: 16 (over z, y, core).
Axes of the slice: x: 2, y: 2, z: 4, core: 2. Of those that a mesh axis runs over, the one named last changes fastest.
Arguments:
- mobile_positions: float32 [512, 3, 128], P(('mob', 'imm')), may hold values from 0 to 4
- walk: float32 [2, 512, 3, 128], P(None, ('mob', 'imm')), may hold values from -1.8 to 1.8
- mobile_conc: float32 [512, 8, 128], P(('mob', 'imm')), may hold values from 0 to 2
- matrix_positions: float32 [512, 3, 128], P(('mob', 'imm')), may hold values from 0 to 4
- matrix_conc: float32 [512, 8, 128], P(('mob', 'imm')), may hold values from 0 to 2
- pair_rows: int32 [2, 16, 512], P('mob', 'imm'), may hold values from 0 to 255, as said below
- pair_cols: int32 [2, 16, 512], P('mob', 'imm'), may hold values from 0 to 31
- pair_counts: int32 [2, 16], P('mob', 'imm'), may hold values from 128 to 512, as said below
Outputs:
- mobile_after: float32 [512, 8, 128], P(('mob', 'imm'))
- matrix_after: float32 [512, 8, 128], P(('mob', 'imm'))
Inputs may be any that keep to these rules, and one draw needn't show every extreme that they name: Within one device the listed pairs (pair_rows, pair_cols) are distinct. `pair_counts`: in every draw some device uses all 512 slots.
All inputs are finite; a program needn't handle non-finite values.
Results may differ from a plain program's by a relative error of at most 0.0003.
Values sent between devices are 32-bit elements; how exact they have to be, the bound alone decides.
A program may use at most 64 MiB of HBM per device.

v0:
```python
import functools
import math

import jax
import jax.numpy as jnp
from jax import lax
from jax.experimental import pallas as pl
from jax.experimental.pallas import tpu as pltpu
from jax.sharding import PartitionSpec as P

RATE = 1.0 / 512.0
SCALE = math.sqrt(0.5 * math.log2(math.e))
CENTRE = 2.0
MESH = pl.DeviceIdType.MESH
VMEM_LIMIT = 48 * 1024 * 1024
UNROLL = 64
GROUPS = 6


class Place:
    def __init__(self, n_mob, n_imm):
        rest = n_imm // 2
        nb = 1
        while nb * nb * 4 <= rest:
            nb *= 2
        self.nm, self.nb, self.na = n_mob, nb, rest // nb
        self.p = lax.axis_index("mob")
        q = lax.axis_index("imm")
        self.core = lax.rem(q, 2)
        chip = lax.div(q, 2)
        self.b = lax.rem(chip, nb)
        self.a = lax.div(chip, nb)

    def am(self, d):
        return lax.rem(self.a + (d + self.na), self.na)

    def bm(self, d):
        return lax.rem(self.b + (d + self.nb), self.nb)

    def pm(self, d):
        return lax.rem(self.p + (d + self.nm), self.nm)

    def dev(self, a, b, core):
        return (self.p, (a * self.nb + b) * 2 + core)

    def sibling(self):
        return self.dev(self.a, self.b, 1 - self.core)

    def across(self, d):
        return (self.pm(d), (self.a * self.nb + self.b) * 2 + self.core)

    def barrier(self):
        sem = pltpu.get_barrier_semaphore()
        peers = [self.sibling()]
        peers += [self.dev(self.a, self.bm(d), self.core) for d in range(1, self.nb)]
        peers += [self.dev(self.am(d), self.b, self.core) for d in range(1, self.na)]
        peers += [self.across(d) for d in range(1, self.nm)]
        for peer in peers:
            pl.semaphore_signal(sem, inc=1, device_id=peer, device_id_type=MESH)
        pl.semaphore_wait(sem, len(peers))


def remote(src, dst, send, recv, device):
    copy = pltpu.make_async_remote_copy(
        src_ref=src, dst_ref=dst, send_sem=send, recv_sem=recv, device_id=device, device_id_type=MESH
    )
    copy.start()
    return copy


def gather_imm(at, refs, sems):
    a_send, a_recv, b_send, b_recv, c_send, c_recv = sems
    na, nb = at.na, at.nb
    sends, a_copies, b_copies, c_copies = [], {}, {}, {}
    for da in range(1, na):
        for i, g in enumerate(refs):
            block = g.at[at.a, at.b, at.core]
            a_copies[da, i] = remote(
                block, block, a_send.at[i, da], a_recv.at[i, da], at.dev(at.am(da), at.b, at.core)
            )
    for da in range(na):
        for i, g in enumerate(refs):
            if da:
                a_copies[da, i].wait_recv()
            block = g.at[at.am(-da), at.b, at.core]
            for db in range(1, nb):
                b_copies[da, db, i] = remote(
                    block, block, b_send.at[i, da, db], b_recv.at[i, da, db], at.dev(at.a, at.bm(db), at.core)
                )
            c_copies[da, 0, i] = remote(
                block, block, c_send.at[i, da, 0], c_recv.at[i, da, 0], at.sibling()
            )
    for da in range(na):
        for db in range(1, nb):
            for i, g in enumerate(refs):
                b_copies[da, db, i].wait_recv()
                block = g.at[at.am(-da), at.bm(-db), at.core]
                c_copies[da, db, i] = remote(
                    block, block, c_send.at[i, da, db], c_recv.at[i, da, db], at.sibling()
                )
    for copy in c_copies.values():
        copy.wait_recv()
    for copies in (a_copies, b_copies, c_copies):
        for copy in copies.values():
            copy.wait_send()


def gather_mob_start(at, refs, send, recv):
    copies = []
    for dp in range(1, at.nm):
        for i, g in enumerate(refs):
            block = g.at[at.p]
            copies.append(remote(block, block, send.at[i, dp], recv.at[i, dp], at.across(dp)))
    return copies


def reduce_mob_start(at, part, land, send, recv):
    return [
        remote(part.at[at.pm(dp)], land.at[dp], send.at[dp], recv.at[dp], at.across(dp))
        for dp in range(1, at.nm)
    ]


def reduce_imm(at, part, land_c, land_b, land_a, out_b, out_a, sems):
    a_send, a_recv, b_send, b_recv, c_send, c_recv = sems
    na, nb = at.na, at.nb
    order = list(range(1, na)) + [0]
    a_copies, b_copies, c_copies = {}, {}, {}
    for db in list(range(1, nb)) + [0]:
        for da in order:
            c_copies[da, db] = remote(
                part.at[at.am(da), at.bm(db), 1 - at.core],
                land_c.at[da, db],
                c_send.at[da, db],
                c_recv.at[da, db],
                at.sibling(),
            )
    for da in order:
        for db in range(1, nb):
            c_copies[da, db].wait_recv()
            out_b[da, db] = part[at.am(da), at.bm(db), at.core] + land_c[da, db]
            b_copies[da, db] = remote(
                out_b.at[da, db],
                land_b.at[da, db],
                b_send.at[da, db],
                b_recv.at[da, db],
                at.dev(at.a, at.bm(db), at.core),
            )
    total = None
    for da in order:
        c_copies[da, 0].wait_recv()
        here = part[at.am(da), at.b, at.core] + land_c[da, 0]
        for db in range(1, nb):
            b_copies[da, db].wait_recv()
            here = here + land_b[da, db]
        if da:
            out_a[da] = here
            a_copies[da] = remote(
                out_a.at[da], land_a.at[da], a_send.at[da], a_recv.at[da], at.dev(at.am(da), at.b, at.core)
            )
        else:
            total = here
    for da in range(1, na):
        a_copies[da].wait_recv()
        total = total + land_a[da]
    for copies in (a_copies, b_copies, c_copies):
        for copy in copies.values():
            copy.wait_send()
    return total


def first_gather(n_mob, n_imm, mpos, walk, mconc, ipos, iconc, g_pos, g_conc, h_pos, h_conc, *sems):
    at = Place(n_mob, n_imm)
    own = g_pos.at[at.a, at.b, at.core]
    moved = mpos[...]
    for step in range(2):
        moved = moved + walk[step]
        x = (moved - CENTRE) * SCALE
        own[:, 4 * step : 4 * step + 3, :] = x
        own[:, 4 * step + 3 : 4 * step + 4, :] = -jnp.sum(x * x, axis=1, keepdims=True)
    g_conc[at.a, at.b, at.core] = mconc[...]
    h_own = h_pos.at[at.p]
    y = (ipos[...] - CENTRE) * SCALE
    h_own[:, 0:3, :] = 2.0 * y
    h_own[:, 3:4, :] = jnp.ones_like(y[:, 0:1, :])
    h_own[:, 4:5, :] = -jnp.sum(y * y, axis=1, keepdims=True)
    h_own[:, 5:8, :] = jnp.zeros_like(y)
    h_conc[at.p] = iconc[...]
    at.barrier()
    mob = gather_mob_start(at, (h_pos, h_conc), *sems[6:])
    gather_imm(at, (g_conc, g_pos), sems[:6])
    for copy in mob:
        copy.wait()


def exchange(n_mob, n_imm, part_m, part_i, conc_m, conc_i, own_m, own_i, g_conc, h_conc,
             land_c, land_b, land_a, out_b, out_a, land_m, *sems):
    at = Place(n_mob, n_imm)
    at.barrier()
    mob = reduce_mob_start(at, part_i, land_m, *sems[6:8])
    total = conc_m[...] + reduce_imm(at, part_m, land_c, land_b, land_a, out_b, out_a, sems[:6])
    own_m[...] = total
    g_conc[at.a, at.b, at.core] = total
    total = conc_i[...] + part_i[at.p]
    for dp, copy in enumerate(mob, 1):
        copy.wait()
        total = total + land_m[dp]
    own_i[...] = total
    h_conc[at.p] = total
    mob = gather_mob_start(at, (h_conc,), *sems[8:10])
    gather_imm(at, (g_conc,), sems[10:16])
    for copy in mob:
        copy.wait()


def last_reduce(n_mob, n_imm, part_m, part_i, conc_m, conc_i, own_m, own_i,
                land_c, land_b, land_a, out_b, out_a, land_m, *sems):
    at = Place(n_mob, n_imm)
    at.barrier()
    mob = reduce_mob_start(at, part_i, land_m, *sems[6:8])
    own_m[...] = conc_m[...] + reduce_imm(at, part_m, land_c, land_b, land_a, out_b, out_a, sems[:6])
    total = conc_i[...] + part_i[at.p]
    for dp, copy in enumerate(mob, 1):
        copy.wait()
        total = total + land_m[dp]
    own_i[...] = total


def split3(x):
    high = x.astype(jnp.bfloat16).astype(jnp.float32)
    rest = x - high
    mid = rest.astype(jnp.bfloat16).astype(jnp.float32)
    return high, mid, rest - mid


def conc_rows(conc):
    high = conc.astype(jnp.bfloat16).astype(jnp.float32)
    ones = jnp.ones_like(conc)
    return jnp.concatenate([high, conc - high, ones, ones], axis=0).astype(jnp.bfloat16)


def pair_loop(step, rows, cols, count, x_pos, x_conc, y_pos, y_conc, gain_m, gain_i, y_split):
    gain_m[...] = jnp.zeros_like(gain_m)
    gain_i[...] = jnp.zeros_like(gain_i)

    def prepare(c, carry):
        h, m, l = split3(y_pos[c])
        zeros = jnp.zeros((128 - 8 * GROUPS, 128), jnp.float32)
        stacked = jnp.concatenate([h, h, h, m, m, l, zeros], axis=0)
        y_split[c] = stacked.T.astype(jnp.bfloat16)
        return carry

    lax.fori_loop(0, y_pos.shape[0], prepare, 0, unroll=8)
    row = lax.broadcasted_iota(jnp.int32, (8, 128), 0)
    keep = row < 4
    unit = jnp.where(row == 4, 1.0, 0.0).astype(jnp.float32)
    zeros = jnp.zeros((128 - 8 * GROUPS, 128), jnp.float32)
    used = count[0, 0]

    def body(block, carry):
        def weigh(u):
            k = block * UNROLL + u
            r, c = rows[0, 0, k], cols[0, 0, k]
            x = x_pos[r]
            if step:
                x = pltpu.roll(x, 4, 0)
            h, m, l = split3(jnp.where(keep, x, unit))
            x_split = jnp.concatenate([h, m, l, h, m, h, zeros], axis=0).astype(jnp.bfloat16)
            power = jnp.dot(y_split[c], x_split, preferred_element_type=jnp.float32)
            return k, r, c, power

        def transfer(k, r, c, power):
            weight = jnp.exp2(power).astype(jnp.bfloat16)
            cm, ci = x_conc[r], y_conc[c]
            to_m = jnp.dot(conc_rows(ci), weight, preferred_element_type=jnp.float32)
            to_i = lax.dot_general(
                conc_rows(cm), weight, (((1,), (1,)), ((), ())), preferred_element_type=jnp.float32
            )
            return k, r, c, cm, ci, to_m, to_i

        def finish(k, r, c, cm, ci, to_m, to_i):
            rate = jnp.where(k < used, RATE, 0.0).astype(jnp.float32)
            add_m = rate * (to_m[0:8] + to_m[8:16] - to_m[16:24] * cm)
            add_i = rate * (to_i[0:8] + to_i[8:16] - to_i[16:24] * ci)
            return r, c, add_m, add_i

        weighed, moved, results = [], [], []
        for u in range(UNROLL + 9):
            if u < UNROLL:
                weighed.append(weigh(u))
            if 5 <= u < UNROLL + 5:
                moved.append(transfer(*weighed[u - 5]))
            if u >= 9:
                results.append(finish(*moved[u - 9]))
        for r, c, add_m, add_i in results:
            gain_m[r] += add_m
            gain_i[c] += add_i
        return carry

    lax.fori_loop(0, lax.div(used + (UNROLL - 1), UNROLL), body, 0)


def on_device(n_mob, n_imm, mpos, walk, mconc, ipos, iconc, rows, cols, counts):
    rest = n_imm // 2
    nb = 1
    while nb * nb * 4 <= rest:
        nb *= 2
    na = rest // nb
    f32 = jnp.float32
    mc, solutes, part = mconc.shape
    ic = iconc.shape[0]
    vmem = pl.BlockSpec(memory_space=pltpu.VMEM)
    smem = pl.BlockSpec(memory_space=pltpu.SMEM)
    dma = pltpu.SemaphoreType.DMA

    def params(ident):
        return pltpu.CompilerParams(collective_id=ident, has_side_effects=True, vmem_limit_bytes=VMEM_LIMIT)

    def gather_sems(refs):
        return [dma((refs, na))] * 2 + [dma((refs, na, nb))] * 4

    reduce_sems = [dma((na,))] * 2 + [dma((na, nb))] * 4
    cell_m = (mc, solutes, part)
    cell_i = (ic, solutes, part)
    all_m = jax.ShapeDtypeStruct((na, nb, 2) + cell_m, f32)
    all_i = jax.ShapeDtypeStruct((n_mob,) + cell_i, f32)
    g_pos, g_conc, h_pos, h_conc = pl.pallas_call(
        functools.partial(first_gather, n_mob, n_imm),
        out_shape=(all_m, all_m, all_i, all_i),
        in_specs=[vmem] * 5,
        out_specs=(vmem,) * 4,
        scratch_shapes=gather_sems(2) + [dma((2, n_mob))] * 2,
        compiler_params=params(0),
    )(mpos, walk, mconc, ipos, iconc)

    flat_m = (n_imm * mc, solutes, part)
    flat_i = (n_mob * ic, solutes, part)

    def pairs(step, x_conc, y_conc):
        gains = pl.pallas_call(
            functools.partial(pair_loop, step),
            out_shape=(jax.ShapeDtypeStruct(flat_m, f32), jax.ShapeDtypeStruct(flat_i, f32)),
            in_specs=[smem] * 3 + [vmem] * 4,
            out_specs=(vmem,) * 2,
            scratch_shapes=[pltpu.VMEM((flat_i[0], part, 128), jnp.bfloat16)],
            compiler_params=pltpu.CompilerParams(vmem_limit_bytes=VMEM_LIMIT),
        )(
            rows,
            cols,
            counts,
            g_pos.reshape(flat_m),
            x_conc.reshape(flat_m),
            h_pos.reshape(flat_i),
            y_conc.reshape(flat_i),
        )
        return gains[0].reshape(all_m.shape), gains[1].reshape(all_i.shape)

    lands = [
        pltpu.VMEM((na, nb) + cell_m, f32),
        pltpu.VMEM((na, nb) + cell_m, f32),
        pltpu.VMEM((na,) + cell_m, f32),
        pltpu.VMEM((na, nb) + cell_m, f32),
        pltpu.VMEM((na,) + cell_m, f32),
        pltpu.VMEM((n_mob,) + cell_i, f32),
    ]
    own = (jax.ShapeDtypeStruct(cell_m, f32), jax.ShapeDtypeStruct(cell_i, f32))
    part_m, part_i = pairs(0, g_conc, h_conc)
    own_m, own_i, g_conc, h_conc = pl.pallas_call(
        functools.partial(exchange, n_mob, n_imm),
        out_shape=own + (all_m, all_i),
        in_specs=[vmem] * 4,
        out_specs=(vmem,) * 4,
        scratch_shapes=lands + reduce_sems + [dma((n_mob,))] * 2 + [dma((1, n_mob))] * 2 + gather_sems(1),
        compiler_params=params(1),
    )(part_m, part_i, mconc, iconc)
    part_m, part_i = pairs(1, g_conc, h_conc)
    return pl.pallas_call(
        functools.partial(last_reduce, n_mob, n_imm),
        out_shape=own,
        in_specs=[vmem] * 4,
        out_specs=(vmem,) * 2,
        scratch_shapes=lands + reduce_sems + [dma((n_mob,))] * 2,
        compiler_params=params(2),
    )(part_m, part_i, own_m, own_i)


def solution(mesh):
    return jax.shard_map(
        functools.partial(on_device, mesh.shape["mob"], mesh.shape["imm"]),
        mesh=mesh,
        in_specs=(
            P(("mob", "imm"), None, None),
            P(None, ("mob", "imm"), None, None),
            P(("mob", "imm"), None, None),
            P(("mob", "imm"), None, None),
            P(("mob", "imm"), None, None),
            P("mob", "imm", None),
            P("mob", "imm", None),
            P("mob", "imm"),
        ),
        out_specs=(P(("mob", "imm"), None, None), P(("mob", "imm"), None, None)),
        check_vma=False,
    )
```

profile of v0, /device:TPU:0, one launch (start us, length us, event | category | flops | bytes accessed | tf_op | source)
XLA Modules:
  0.0 103.8 jit_solution(7115559174712265961)
XLA Ops:
  0.6 0.0 copy-start.5
  1.3 0.0 copy-start.4
  1.3 0.8 copy.10.mpos
  2.1 0.0 copy-done.5
  2.1 0.0 copy-start.1
  2.1 0.0 copy-done.4
  2.1 0.0 copy-start
  2.2 0.8 copy-done.1
  2.9 0.1 copy-done
  3.0 22.5 %shard_map.95 = (f32[4,2,2,16,8,128]{5,4,3,2,1,0:T(8,128)S(1)}, f32[4,2,2,16,8,128]{5,4,3,2,1,0:T(8,128)S(1)}, f32[2,16,8,128]{3,2,1,0:T(8,128)S(1)}, f32[2,16,8,128]{3,2,1,0:T(8,128)S(1)}) custom-call(f32[16,3,128]{2,1,0:T(4,128)S(1)} %copy.10.mpos, f32[2,16,3,128]{3,2,1,0:T(4,128)S(1)} %copy.11.walk, f32[16,8,128]{2,1,0:T(8,128)S(1)} %copy-done, ...), custom_call_target="tpu_custom_call" | custom-call | tf_op jit(solution)/shard_map/pallas_call | solution.py:327
  25.5 0.0 copy-start.3
  25.5 0.0 copy-start.2
  25.5 0.7 copy-done.3
  26.2 0.0 copy-done.2
  26.2 10.0 %shard_map.96 = (f32[256,8,128]{2,1,0:T(8,128)S(1)}, f32[32,8,128]{2,1,0:T(8,128)S(1)}) custom-call(s32[1,1,512]{2,1,0:T(1,128)S(1)} %copy-done.2, s32[1,1,512]{2,1,0:T(1,128)S(1)} %copy-done.3, s32[1,1]{1,0:T(1,128)S(6)} %copy.15.count, f32[256,8,128]{2,1,0:T(8,128)S(1)} %bitcast.10, f32[256,8,128]{2,1,0:T(8,128)S(1)} %bitcast.15, ...), custom_call_target="tpu_custom_call" | custom-call | tf_op jit(solution)/shard_map/pallas_call | solution.py:340
  36.2 32.3 %shard_map.97 = (f32[16,8,128]{2,1,0:T(8,128)S(1)}, f32[16,8,128]{2,1,0:T(8,128)S(1)}, f32[4,2,2,16,8,128]{5,4,3,2,1,0:T(8,128)S(1)}, f32[2,16,8,128]{3,2,1,0:T(8,128)S(1)}) custom-call(f32[4,2,2,16,8,128]{5,4,3,2,1,0:T(8,128)S(1)} %bitcast.13, f32[2,16,8,128]{3,2,1,0:T(8,128)S(1)} %bitcast.19, f32[16,8,128]{2,1,0:T(8,128)S(1)} %copy-done, ...), custom_call_target="tpu_custom_call" | custom-call | tf_op jit(solution)/shard_map/pallas_call | solution.py:368
  68.5 10.0 %shard_map.98 = (f32[256,8,128]{2,1,0:T(8,128)S(1)}, f32[32,8,128]{2,1,0:T(8,128)S(1)}) custom-call(s32[1,1,512]{2,1,0:T(1,128)S(1)} %copy-done.2, s32[1,1,512]{2,1,0:T(1,128)S(1)} %copy-done.3, s32[1,1]{1,0:T(1,128)S(6)} %copy.15.count, f32[256,8,128]{2,1,0:T(8,128)S(1)} %bitcast.11, f32[256,8,128]{2,1,0:T(8,128)S(1)} %bitcast.14, ...), custom_call_target="tpu_custom_call" | custom-call | tf_op jit(solution)/shard_map/pallas_call | solution.py:340
  78.5 24.1 %shard_map.99 = (f32[16,8,128]{2,1,0:T(8,128)S(1)}, f32[16,8,128]{2,1,0:T(8,128)S(1)}) custom-call(f32[4,2,2,16,8,128]{5,4,3,2,1,0:T(8,128)S(1)} %bitcast.12, f32[2,16,8,128]{3,2,1,0:T(8,128)S(1)} %bitcast.18, f32[16,8,128]{2,1,0:T(8,128)S(1)} %get-tuple-element.24.conc_m, f32[16,8,128]{2,1,0:T(8,128)S(1)} %get-tuple-element.25.conc_i), custom_call_target="tpu_custom_call" | custom-call | tf_op jit(solution)/shard_map/pallas_call | solution.py:377
  102.6 0.6 copy.16
  103.2 0.6 copy.17
  (2 shorter events, 0.0 us)
Async XLA Ops:
  0.6 1.4 %copy-start.5 = (f32[16,3,128]{2,0,1:T(8,128)S(1)}, f32[16,3,128]{2,0,1:T(8,128)}, u32[]{:S(2)}) copy-start(f32[16,3,128]{2,0,1:T(8,128)} %param.11) | copy-start | bytes 73732
  1.3 0.8 copy-start.4
  2.1 0.8 copy-start.1
  2.1 0.8 copy-start
  25.5 0.7 copy-start.3
  25.5 0.7 copy-start.2
where the time goes:
time: 106 us; the launch traced here: 104 us
  Pallas kernels  98.8 us (93%)
  local copies, waits for them, and re-layouts  3.57 us (3%)
  between operations  1.39 us (1%)
    pallas_call x1, Pallas kernels, on_device(): pl.pallas_call(functools.partial(exchange, n_mob, n_imm), out_shape=own +...  32.3 us
    pallas_call x1, Pallas kernels, on_device(): pl.pallas_call(functools.partial(last_reduce, n_mob, n_imm), out_shape=ow...  24.1 us
    pallas_call x1, Pallas kernels, on_device(): pl.pallas_call(functools.partial(first_gather, n_mob, n_imm), out_shape=(...  22.5 us
    pallas_call x2, Pallas kernels, pairs(): pl.pallas_call(functools.partial(pair_loop, step), out_shape=(jax.ShapeDt...  19.9 us
    unnamed x17, local copies, waits for them, and re-layouts  3.57 us

commit v1 on v0

v1 whole, which is shorter than its diff:
```python
import functools
import math

import jax
import jax.numpy as jnp
from jax import lax
from jax.experimental import pallas as pl
from jax.experimental.pallas import tpu as pltpu
from jax.sharding import PartitionSpec as P

RATE = 1.0 / 512.0
SCALE = math.sqrt(0.5 * math.log2(math.e))
CENTRE = 2.0
FAR = -30000.0
MESH = pl.DeviceIdType.MESH
VMEM_LIMIT = 56 * 1024 * 1024
UNROLL = 8
TERMS = 16
F32 = jnp.float32
BF16 = jnp.bfloat16


def sizes(n_mob, n_imm):
    rest = n_imm // 2
    nb = 1
    while nb * nb * 4 <= rest:
        nb *= 2
    return n_mob, nb, rest // nb


class Place:
    def __init__(self, n_mob, n_imm):
        self.nm, self.nb, self.na = sizes(n_mob, n_imm)
        self.p = lax.axis_index("mob")
        q = lax.axis_index("imm")
        self.core = lax.rem(q, 2)
        chip = lax.div(q, 2)
        self.b = lax.rem(chip, self.nb)
        self.a = lax.div(chip, self.nb)

    def am(self, d):
        return lax.rem(self.a + (d + self.na), self.na)

    def bm(self, d):
        return lax.rem(self.b + (d + self.nb), self.nb)

    def pm(self, d):
        return lax.rem(self.p + (d + self.nm), self.nm)

    def dev(self, p, a, b, core):
        return (p, (a * self.nb + b) * 2 + core)

    def along(self, da):
        return self.dev(self.p, self.am(da), self.b, self.core)

    def across(self, dp, db):
        return self.dev(self.pm(dp), self.a, self.bm(db), self.core)

    def sibling(self):
        return self.dev(self.p, self.a, self.b, 1 - self.core)

    def plane(self):
        return [(dp, db) for dp in range(self.nm) for db in range(self.nb) if dp or db]

    def slot(self, dp, db, core):
        return (self.pm(dp) * self.nb + self.bm(db)) * 2 + core

    def greet(self, lists=False):
        sem = pltpu.get_barrier_semaphore()
        peers = [self.sibling()]
        peers += [self.along(d) for d in range(1, self.na)]
        peers += [self.across(dp, db) for dp, db in self.plane()]
        if lists:
            peers += [self.dev(self.p, self.a, self.bm(db), 1 - self.core) for db in range(1, self.nb)]
        for peer in peers:
            pl.semaphore_signal(sem, inc=1, device_id=peer, device_id_type=MESH)
        return sem, len(peers)


def remote(src, dst, sems, index, device):
    copy = pltpu.make_async_remote_copy(
        src_ref=src, dst_ref=dst, send_sem=sems[0].at[index], recv_sem=sems[1].at[index],
        device_id=device, device_id_type=MESH,
    )
    copy.start()
    return copy


def split2(x):
    high = x.astype(BF16).astype(F32)
    return high, x - high


def split3(x):
    high, rest = split2(x)
    mid, low = split2(rest)
    return high, mid, low


def rows_x(x):
    (xh, xm), (yh, ym), (zh, zm) = [split2(x[j]) for j in range(3)]
    norm = split3(-(x[0] * x[0] + x[1] * x[1] + x[2] * x[2]))
    one = jnp.ones_like(x[0])
    return [xh, yh, zh, xh, yh, zh, xm, ym, zm, *norm, one, one, one, jnp.zeros_like(one)]


def rows_y(y):
    (xh, xm), (yh, ym), (zh, zm) = [split2(2.0 * y[j]) for j in range(3)]
    norm = split3(-(y[0] * y[0] + y[1] * y[1] + y[2] * y[2]))
    one = jnp.ones_like(y[0])
    return [xh, yh, zh, xm, ym, zm, xh, yh, zh, one, one, one, *norm, jnp.zeros_like(one)]


def fill(stage, rows):
    cells = rows[0].shape[0]
    for j, row in enumerate(rows):
        stage[pl.ds(j, cells, stride=TERMS), :] = row


def build_y(pos, stage, out, slot):
    cells = pos.shape[1]
    fill(stage, rows_y([pos[j] for j in range(3)]))
    out[pl.ds(slot * cells, cells)] = stage[...].reshape(cells, TERMS, 128).astype(BF16)


def build_x(pos, stage, out, slot):
    cells = pos.shape[1]
    fill(stage, rows_x([pos[j] for j in range(3)]))
    zeros = jnp.zeros((128 - TERMS, 128), F32)
    for cell in range(cells):
        block = jnp.concatenate([stage[cell * TERMS : (cell + 1) * TERMS, :], zeros], axis=0)
        out[slot * cells + cell] = block.T.astype(BF16)


def build_list(at, mc, ic, lists, keep_m, keep_i, keep_rank, out):
    lists_n, chunks = lists.shape[0], lists.shape[0] * 4
    cells_m = at.na * mc
    lines = (out.shape[0] - 8) // 3
    shift_m, shift_i, shift_b = [int(math.log2(n)) for n in (mc, ic, at.nb)]
    lane = lax.broadcasted_iota(jnp.int32, (1, 128), 1)
    mine = lax.broadcasted_iota(jnp.int32, (cells_m, 128), 0)
    upper = jnp.where(
        lax.broadcasted_iota(jnp.int32, (128, 128), 0) <= lax.broadcasted_iota(jnp.int32, (128, 128), 1), 1.0, 0.0
    ).astype(BF16)
    lower = jnp.where(
        lax.broadcasted_iota(jnp.int32, (cells_m, cells_m), 0)
        > lax.broadcasted_iota(jnp.int32, (cells_m, cells_m), 1), 1.0, 0.0
    ).astype(F32)

    def count(chunk, total):
        which, part = lax.div(chunk, 4), lax.rem(chunk, 4)
        r = lists[which, pl.ds(part, 1), :]
        c = lists[which, pl.ds(4 + part, 1), :]
        used = lists[which, 8:9, :]
        owner = jnp.right_shift(r, shift_m)
        ok = (
            (part * 128 + lane < used)
            & (jnp.bitwise_and(owner, 1) == at.core)
            & (jnp.bitwise_and(jnp.right_shift(owner, 1), at.nb - 1) == at.b)
        )
        m = jnp.right_shift(owner, 1 + shift_b) * mc + jnp.bitwise_and(r, mc - 1)
        m = jnp.where(ok, m, -1)
        i = (jnp.right_shift(c, shift_i) * lists_n + which) * ic + jnp.bitwise_and(c, ic - 1)
        hot = jnp.where(mine == m, 1.0, 0.0).astype(F32)
        rank = total + jnp.dot(hot.astype(BF16), upper, preferred_element_type=F32)
        keep_m[pl.ds(chunk, 1), :] = m
        keep_i[pl.ds(chunk, 1), :] = i + 1
        keep_rank[pl.ds(chunk, 1), :] = jnp.sum(hot * rank, axis=0, keepdims=True) - 1.0
        return jnp.broadcast_to(rank[:, 127:128], rank.shape)

    total = lax.fori_loop(0, chunks, count, jnp.zeros((cells_m, 128), F32))
    even = 2.0 * jnp.floor((total + 1.0) * 0.5)
    start = jnp.dot(lower, even, preferred_element_type=F32, precision=lax.Precision.HIGHEST)
    doubles = jnp.sum(even, axis=0, keepdims=True) * 0.5
    line = lax.broadcasted_iota(jnp.int32, (lines, 128), 0)
    column = lax.broadcasted_iota(jnp.int32, (128, 128), 0)

    def place(chunk, acc):
        m = keep_m[pl.ds(chunk, 1), :]
        i = keep_i[pl.ds(chunk, 1), :]
        hot = jnp.where(mine == m, 1.0, 0.0).astype(F32)
        spot = jnp.sum(hot * start, axis=0, keepdims=True) + keep_rank[pl.ds(chunk, 1), :]
        spot = jnp.where(m >= 0, spot.astype(jnp.int32), -1)
        double = jnp.right_shift(spot, 1)
        second = jnp.bitwise_and(spot, 1) == 1
        here = (line == jnp.right_shift(double, 7)) & (m >= 0)
        lane_hot = jnp.where(column == jnp.bitwise_and(double, 127), 1.0, 0.0).astype(BF16)
        high = jnp.right_shift(i, 6).astype(F32)
        low = jnp.bitwise_and(i, 63).astype(F32)
        zero = jnp.zeros((1, 128), F32)
        values = [
            jnp.where(second, zero, m.astype(F32)),
            jnp.where(second, zero, high),
            jnp.where(second, zero, low),
            jnp.where(second, high, zero),
            jnp.where(second, low, zero),
        ]
        left = jnp.concatenate([jnp.where(here, v, 0.0) for v in values], axis=0).astype(BF16)
        return acc + lax.dot_general(left, lane_hot, (((1,), (1,)), ((), ())), preferred_element_type=F32)

    acc = lax.fori_loop(0, chunks, place, jnp.zeros((5 * lines, 128), F32))
    m, high1, low1, high2, low2 = [
        acc[j * lines : (j + 1) * lines].astype(jnp.int32) for j in range(5)
    ]
    dummy = at.nm * lists_n * ic
    out[0:lines, :] = m
    for j, (high, low) in enumerate(((high1, low1), (high2, low2)), 1):
        i = high * 64 + low
        out[j * lines : (j + 1) * lines, :] = jnp.where(i == 0, dummy, i - 1)
    out[3 * lines : 3 * lines + 8, :] = jnp.broadcast_to(doubles.astype(jnp.int32), (8, 128))


def gather_plane_start(at, ref, own, sems):
    return {
        (dp, db): remote(own, ref.at[at.slot(0, 0, at.core)], sems, (dp, db), at.across(dp, db))
        for dp, db in at.plane()
    }


def pass_on(at, ref, sems, dp, db, source=None):
    block = ref.at[at.slot(-dp, -db, at.core)]
    return remote(block if source is None else source, block, sems, (dp, db), at.sibling())


def first_gather(n_mob, n_imm, mpos, walk, mconc, ipos, iconc, rows, cols, count,
                 g_conc, h_conc, x_one, y_all, pair_list, x_two,
                 g_pos, h_pos, lists, in_m, in_w, in_i, in_r, in_c, stage, keep_m, keep_i, keep_rank, *sems):
    at = Place(n_mob, n_imm)
    local, z_pos, z_conc, x_pos, x_conc, c_pos, c_conc, l_sem = (
        sems[0], sems[1:3], sems[3:5], sems[5:7], sems[7:9], sems[9:11], sems[11:13], sems[13:15])
    me = at.slot(0, 0, at.core)
    reads = [
        pltpu.make_async_copy(src, dst, local.at[j])
        for j, (src, dst) in enumerate((
            (mpos, in_m), (walk, in_w), (ipos, in_i), (rows, in_r), (cols, in_c),
            (mconc, g_conc.at[at.a]), (iconc, h_conc.at[me]),
        ))
    ]
    for read in reads:
        read.start()
    sem, peers = at.greet(lists=True)
    reads[0].wait()
    reads[1].wait()
    moved = in_m[...] + in_w[0]
    g_pos[at.a] = (moved - CENTRE) * SCALE
    x_two[...] = ((moved + in_w[1]) - CENTRE) * SCALE
    reads[2].wait()
    h_pos[me] = (in_i[...] - CENTRE) * SCALE
    reads[3].wait()
    reads[4].wait()
    home = at.b * 2 + at.core
    for j in range(4):
        lists[home, j : j + 1, :] = in_r[0, :, j * 128 : (j + 1) * 128]
        lists[home, 4 + j : 5 + j, :] = in_c[0, :, j * 128 : (j + 1) * 128]
    lists[home, 8:16, :] = jnp.full((8, 128), count[0, 0], jnp.int32)
    pl.semaphore_wait(sem, peers)
    order = list(range(1, at.na))
    far = {}
    for da in order:
        far[da] = remote(g_pos.at[at.a], g_pos.at[at.a], z_pos, da, at.along(da))
    share = []
    for db in range(at.nb):
        for dc in range(2):
            if db or dc:
                core = at.core if dc == 0 else 1 - at.core
                share.append(remote(
                    lists.at[home], lists.at[home], l_sem, (db, dc), at.dev(at.p, at.a, at.bm(db), core)))
    p_copies = gather_plane_start(at, h_pos, h_pos.at[me], x_pos)
    for da in order:
        far[at.na + da] = remote(mconc, g_conc.at[at.a], z_conc, da, at.along(da))
    q_copies = gather_plane_start(at, h_conc, iconc, x_conc)
    p_pass = {(0, 0): pass_on(at, h_pos, c_pos, 0, 0)}
    q_pass = {(0, 0): pass_on(at, h_conc, c_conc, 0, 0, iconc)}
    for copy in share:
        copy.wait_recv()
    build_x(g_pos.at[at.a], stage, x_one, at.a)
    build_y(h_pos.at[me], stage, y_all, me)
    build_list(at, mconc.shape[0], iconc.shape[0], lists, keep_m, keep_i, keep_rank, pair_list)
    for dp, db in at.plane():
        p_copies[dp, db].wait_recv()
        p_pass[dp, db] = pass_on(at, h_pos, c_pos, dp, db)
        here = at.slot(-dp, -db, at.core)
        build_y(h_pos.at[here], stage, y_all, here)
    cells_i = y_all.shape[0] - 8
    row = lax.broadcasted_iota(jnp.int32, (8, TERMS, 128), 1)
    y_all[cells_i:, :, :] = jnp.where(row == 12, FAR, 0.0).astype(BF16)
    for dp, db in at.plane():
        q_copies[dp, db].wait_recv()
        q_pass[dp, db] = pass_on(at, h_conc, c_conc, dp, db)
    for (dp, db), copy in p_pass.items():
        copy.wait_recv()
        there = at.slot(-dp, -db, 1 - at.core)
        build_y(h_pos.at[there], stage, y_all, there)
    for da in order:
        far[da].wait_recv()
        build_x(g_pos.at[at.am(-da)], stage, x_one, at.am(-da))
    for copy in q_pass.values():
        copy.wait_recv()
    for da in order:
        far[at.na + da].wait_recv()
    for read in reads[5:]:
        read.wait()
    for group in (far, p_copies, q_copies, p_pass, q_pass):
        for copy in group.values():
            copy.wait_send()
    for copy in share:
        copy.wait_send()


def reduce_start(at, part_m, part_i, land_m, land_c, z_sem, c_sem):
    mc = land_m.shape[1]
    ic = land_c.shape[2]
    z_copies, c_copies = {}, {}
    for da in range(1, at.na):
        z_copies[da] = remote(
            part_m.at[pl.ds(at.am(da) * mc, mc)], land_m.at[da], z_sem, da, at.along(da))
    for dp, db in at.plane() + [(0, 0)]:
        c_copies[dp, db] = remote(
            part_i.at[pl.ds(at.slot(dp, db, 1 - at.core) * ic, ic)], land_c.at[dp, db], c_sem, (dp, db), at.sibling())
    return z_copies, c_copies


def reduce_plane_start(at, part_i, land_c, out_b, land_b, c_copies, b_sem):
    ic = land_c.shape[2]
    b_copies = {}
    for dp, db in at.plane():
        c_copies[dp, db].wait_recv()
        out_b[dp, db] = part_i[pl.ds(at.slot(dp, db, at.core) * ic, ic)] + land_c[dp, db]
        b_copies[dp, db] = remote(out_b.at[dp, db], land_b.at[dp, db], b_sem, (dp, db), at.across(dp, db))
    return b_copies


def reduce_m(at, part_m, land_m, z_copies):
    mc = land_m.shape[1]
    total = part_m[pl.ds(at.a * mc, mc)]
    for da, copy in z_copies.items():
        copy.wait_recv()
        total = total + land_m[da]
    return total


def reduce_i(at, part_i, land_c, land_b, c_copies, b_copies):
    ic = land_c.shape[2]
    c_copies[0, 0].wait_recv()
    total = part_i[pl.ds(at.slot(0, 0, at.core) * ic, ic)] + land_c[0, 0]
    for key, copy in b_copies.items():
        copy.wait_recv()
        total = total + land_b[key]
    return total


def exchange(n_mob, n_imm, part_m, part_i, conc_m, conc_i, x_two, own_m, own_i, g_conc, h_conc, x_all,
             land_m, land_c, out_b, land_b, g_pos, stage, *sems):
    at = Place(n_mob, n_imm)
    z_sem, c_sem, b_sem, z_pos, z_conc, x_conc, c_conc = [sems[j : j + 2] for j in range(0, 14, 2)]
    sem, peers = at.greet()
    build_x(x_two, stage, x_all, at.a)
    pl.semaphore_wait(sem, peers)
    z_copies, c_copies = reduce_start(at, part_m, part_i, land_m, land_c, z_sem, c_sem)
    b_copies = reduce_plane_start(at, part_i, land_c, out_b, land_b, c_copies, b_sem)
    far = {}
    for da in range(1, at.na):
        far[da] = remote(x_two, g_pos.at[da], z_pos, da, at.along(da))
    me = at.slot(0, 0, at.core)
    own_i[...] = conc_i[...] + reduce_i(at, part_i, land_c, land_b, c_copies, b_copies)
    q_copies = gather_plane_start(at, h_conc, own_i, x_conc)
    q_pass = {(0, 0): pass_on(at, h_conc, c_conc, 0, 0, own_i)}
    h_conc[me] = own_i[...]
    own_m[...] = conc_m[...] + reduce_m(at, part_m, land_m, z_copies)
    for da in range(1, at.na):
        far[at.na + da] = remote(own_m, g_conc.at[at.a], z_conc, da, at.along(da))
    g_conc[at.a] = own_m[...]
    for da in range(1, at.na):
        far[da].wait_recv()
        build_x(g_pos.at[da], stage, x_all, at.am(-da))
    for dp, db in at.plane():
        q_copies[dp, db].wait_recv()
        q_pass[dp, db] = pass_on(at, h_conc, c_conc, dp, db)
    for copy in q_pass.values():
        copy.wait_recv()
    for da in range(1, at.na):
        far[at.na + da].wait_recv()
    for group in (z_copies, c_copies, b_copies, far, q_copies, q_pass):
        for copy in group.values():
            copy.wait_send()


def last_reduce(n_mob, n_imm, part_m, part_i, conc_m, conc_i, own_m, own_i,
                land_m, land_c, out_b, land_b, *sems):
    at = Place(n_mob, n_imm)
    z_sem, c_sem, b_sem = [sems[j : j + 2] for j in range(0, 6, 2)]
    sem, peers = at.greet()
    pl.semaphore_wait(sem, peers)
    z_copies, c_copies = reduce_start(at, part_m, part_i, land_m, land_c, z_sem, c_sem)
    b_copies = reduce_plane_start(at, part_i, land_c, out_b, land_b, c_copies, b_sem)
    own_i[...] = conc_i[...] + reduce_i(at, part_i, land_c, land_b, c_copies, b_copies)
    own_m[...] = conc_m[...] + reduce_m(at, part_m, land_m, z_copies)
    for group in (z_copies, c_copies, b_copies):
        for copy in group.values():
            copy.wait_send()


def conc_rows(conc):
    conc = conc * RATE
    high = conc.astype(BF16).astype(F32)
    ones = jnp.full_like(conc, RATE)
    return jnp.concatenate([high, conc - high, ones, ones], axis=0).astype(BF16)


def pair_loop(pair_list, x_all, y_all, x_conc, y_conc, gain_m, gain_i, lst, w_even, w_odd, m_rows, i_rows, sem):
    read = pltpu.make_async_copy(pair_list, lst, sem)
    read.start()
    gain_m[...] = jnp.zeros_like(gain_m)
    gain_i[...] = jnp.zeros_like(gain_i)
    w_odd[...] = jnp.zeros_like(w_odd)
    cells_i = y_conc.shape[0]

    def prepare_m(c, carry):
        m_rows[c] = conc_rows(x_conc[c])
        return carry

    def prepare_i(c, carry):
        i_rows[c] = conc_rows(y_conc[c])
        return carry

    lax.fori_loop(0, x_conc.shape[0], prepare_m, 0, unroll=8)
    lax.fori_loop(0, cells_i, prepare_i, 0, unroll=8)
    i_rows[cells_i] = jnp.zeros((32, 128), BF16)
    read.wait()
    lines = (lst.shape[0] - 8) // 3
    used = lst[3 * lines, 0]

    def entry(block, u):
        spot = block * UNROLL
        line, lane = lax.div(spot, 128), lax.rem(spot, 128) + u
        return lst[line, lane], lst[lines + line, lane], lst[2 * lines + line, lane]

    def weigh(block, u, out):
        m, i, k = entry(block, u)
        right = jnp.concatenate([y_all[i], y_all[k]], axis=1)
        power = jnp.dot(x_all[m][:, :TERMS], right, preferred_element_type=F32)
        out[u] = jnp.exp2(power).astype(BF16)

    def transfer(block, u, weights):
        m, i, k = entry(block, u)
        weight = weights[u]
        to_i = jnp.dot(m_rows[m], weight, preferred_element_type=F32)
        right = jnp.concatenate([i_rows[i], i_rows[k]], axis=1)
        to_m = lax.dot_general(right, weight, (((1,), (1,)), ((), ())), preferred_element_type=F32)
        return m, i, k, to_i, to_m

    def finish(m, i, k, to_i, to_m):
        gain_m[m] += to_m[0:8] + to_m[8:16] - to_m[16:24] * x_conc[m]
        add_i = to_i[0:8, :128] + to_i[8:16, :128] - to_i[16:24, :128] * y_conc[jnp.minimum(i, cells_i - 1)]
        add_k = to_i[0:8, 128:] + to_i[8:16, 128:] - to_i[16:24, 128:] * y_conc[jnp.minimum(k, cells_i - 1)]
        gain_i[i] += add_i
        gain_i[k] += add_k

    def half(block, out, weights):
        before = jnp.maximum(block - 1, 0)
        moved = []
        for u in range(UNROLL):
            moved.append(transfer(before, u, weights))
            weigh(block, u, out)
        for item in moved:
            finish(*item)

    def body(t, carry):
        half(2 * t, w_even, w_odd)
        half(2 * t + 1, w_odd, w_even)
        return carry

    blocks = lax.div(used + (UNROLL - 1), UNROLL)
    lax.fori_loop(0, lax.div(blocks + 2, 2), body, 0)


def on_device(n_mob, n_imm, mpos, walk, mconc, ipos, iconc, rows, cols, counts):
    nm, nb, na = sizes(n_mob, n_imm)
    mc, solutes, part = mconc.shape
    ic = iconc.shape[0]
    slots = nm * nb * 2
    cells_m, cells_i = na * mc, slots * ic
    tiles = nb * 2
    chunks = tiles * 4
    lines = -(-(chunks * 64 + cells_m // 2 + 4 * UNROLL) // 128)
    lines = -(-lines // 16) * 16
    vmem = pl.BlockSpec(memory_space=pltpu.VMEM)
    smem = pl.BlockSpec(memory_space=pltpu.SMEM)
    anywhere = pl.BlockSpec(memory_space=pl.ANY)
    dma = pltpu.SemaphoreType.DMA

    def params(ident):
        return pltpu.CompilerParams(collective_id=ident, has_side_effects=True, vmem_limit_bytes=VMEM_LIMIT)

    def shape(dims, dtype=F32):
        return jax.ShapeDtypeStruct(dims, dtype)

    def pairs(*dims):
        return [dma(dims)] * 2

    cell_m, cell_i = (mc, solutes, part), (ic, solutes, part)
    all_m, all_i = (na,) + cell_m, (slots,) + cell_i
    pos_m, pos_i = (3, mc, part), (3, ic, part)
    stage = pltpu.VMEM((max(mc, ic) * TERMS, part), F32)
    x_shape = shape((cells_m, part, 128), BF16)
    g_conc, h_conc, x_one, y_all, pair_list, x_two = pl.pallas_call(
        functools.partial(first_gather, n_mob, n_imm),
        out_shape=(
            shape(all_m), shape(all_i), x_shape, shape((cells_i + 8, TERMS, part), BF16),
            shape((3 * lines + 8, 128), jnp.int32), shape(pos_m),
        ),
        in_specs=[anywhere] * 7 + [smem],
        out_specs=(vmem,) * 6,
        scratch_shapes=[
            pltpu.VMEM((na,) + pos_m, F32), pltpu.VMEM((slots,) + pos_i, F32),
            pltpu.VMEM((tiles, 16, 128), jnp.int32),
            pltpu.VMEM(pos_m, F32), pltpu.VMEM((2,) + pos_m, F32), pltpu.VMEM(pos_i, F32),
            pltpu.VMEM(rows.shape, jnp.int32), pltpu.VMEM(cols.shape, jnp.int32), stage,
            pltpu.VMEM((chunks, 128), jnp.int32), pltpu.VMEM((chunks, 128), jnp.int32),
            pltpu.VMEM((chunks, 128), F32),
            dma((7,)), *pairs(na), *pairs(na), *pairs(nm, nb), *pairs(nm, nb), *pairs(nm, nb), *pairs(nm, nb),
            *pairs(nb, 2),
        ],
        compiler_params=params(0),
    )(jnp.transpose(mpos, (1, 0, 2)), jnp.transpose(walk, (0, 2, 1, 3)), mconc,
      jnp.transpose(ipos, (1, 0, 2)), iconc, rows, cols, counts)

    def gains(x_all, x_conc, y_conc):
        return pl.pallas_call(
            pair_loop,
            out_shape=(shape((cells_m, solutes, part)), shape((cells_i + 1, solutes, part))),
            in_specs=[anywhere] + [vmem] * 4,
            out_specs=(vmem,) * 2,
            scratch_shapes=[
                pltpu.SMEM(pair_list.shape, jnp.int32),
                pltpu.VMEM((UNROLL, part, 256), BF16), pltpu.VMEM((UNROLL, part, 256), BF16),
                pltpu.VMEM((cells_m, 32, part), BF16), pltpu.VMEM((cells_i + 1, 32, part), BF16),
                dma,
            ],
            compiler_params=pltpu.CompilerParams(vmem_limit_bytes=VMEM_LIMIT),
        )(pair_list, x_all, y_all,
          x_conc.reshape((cells_m, solutes, part)), y_conc.reshape((cells_i, solutes, part)))

    lands = [
        pltpu.VMEM((na,) + cell_m, F32),
        pltpu.VMEM((nm, nb) + cell_i, F32), pltpu.VMEM((nm, nb) + cell_i, F32), pltpu.VMEM((nm, nb) + cell_i, F32),
    ]
    reduce_sems = [*pairs(na), *pairs(nm, nb), *pairs(nm, nb)]
    own = (shape(cell_m), shape(cell_i))
    part_m, part_i = gains(x_one, g_conc, h_conc)
    own_m, own_i, g_conc, h_conc, x_all = pl.pallas_call(
        functools.partial(exchange, n_mob, n_imm),
        out_shape=own + (shape(all_m), shape(all_i), x_shape),
        in_specs=[vmem] * 5,
        out_specs=(vmem,) * 5,
        scratch_shapes=lands + [pltpu.VMEM((na,) + pos_m, F32), stage] + reduce_sems + [
            *pairs(na), *pairs(na), *pairs(nm, nb), *pairs(nm, nb)],
        compiler_params=params(1),
    )(part_m, part_i, mconc, iconc, x_two)
    part_m, part_i = gains(x_all, g_conc, h_conc)
    return pl.pallas_call(
        functools.partial(last_reduce, n_mob, n_imm),
        out_shape=own,
        in_specs=[vmem] * 4,
        out_specs=(vmem,) * 2,
        scratch_shapes=lands + reduce_sems,
        compiler_params=params(2),
    )(part_m, part_i, own_m, own_i)


def solution(mesh):
    return jax.shard_map(
        functools.partial(on_device, mesh.shape["mob"], mesh.shape["imm"]),
        mesh=mesh,
        in_specs=(
            P(("mob", "imm"), None, None),
            P(None, ("mob", "imm"), None, None),
            P(("mob", "imm"), None, None),
            P(("mob", "imm"), None, None),
            P(("mob", "imm"), None, None),
            P("mob", "imm", None),
            P("mob", "imm", None),
            P("mob", "imm"),
        ),
        out_specs=(P(("mob", "imm"), None, None), P(("mob", "imm"), None, None)),
        check_vma=False,
    )
```

time: 106 us -> 78.6 us (0.74); the launches traced: 104 us -> 78.5 us
  Pallas kernels: 98.8 us -> 74.2 us
    pallas_call x1, Pallas kernels: 32.3 us -> 20.3 us  [on_device(): pl.pallas_call(functools.partial(exchange, n_mob, n_imm), out_shape=own +...]
    pallas_call x1, Pallas kernels: 24.1 us -> 13.8 us  [on_device(): pl.pallas_call(functools.partial(last_reduce, n_mob, n_imm), out_shape=ow...]
    pallas_call x1, Pallas kernels: 22.5 us -> 19.4 us  [on_device(): pl.pallas_call(functools.partial(first_gather, n_mob, n_imm), out_shape=(...]
    unnamed x17 -> x2, local copies, waits for them, and re-layouts: 3.57 us -> 2.95 us
where the time goes in v1:
time: 78.6 us; the launch traced here: 78.5 us
  Pallas kernels  74.2 us (94%)
  local copies, waits for them, and re-layouts  2.95 us (4%)
  between operations  1.32 us (2%)
    pallas_call x2, Pallas kernels, gains(): pl.pallas_call(pair_loop, out_shape=(shape((cells_m, solutes, part)), sha...  20.7 us
    pallas_call x1, Pallas kernels, on_device(): pl.pallas_call(functools.partial(exchange, n_mob, n_imm), out_shape=own +...  20.3 us
    pallas_call x1, Pallas kernels, on_device(): pl.pallas_call(functools.partial(first_gather, n_mob, n_imm), out_shape=(...  19.4 us
    pallas_call x1, Pallas kernels, on_device(): pl.pallas_call(functools.partial(last_reduce, n_mob, n_imm), out_shape=ow...  13.8 us
    unnamed x2, local copies, waits for them, and re-layouts  2.95 us

profile of v1, /device:TPU:0, one launch (start us, length us, event | category | flops | bytes accessed | tf_op | source)
XLA Modules:
  0.0 78.5 jit_solution(4626822231768732493)
XLA Ops:
  1.3 19.4 %shard_map.95 = (f32[4,16,8,128]{3,2,1,0:T(8,128)}, f32[8,16,8,128]{3,2,1,0:T(8,128)}, bf16[64,128,128]{2,1,0:T(8,128)(2,1)}, bf16[136,16,128]{2,1,0:T(8,128)(2,...) custom-call(f32[3,16,128]{2,1,0:T(8,128)} %bitcast.12, f32[2,3,16,128]{3,2,1,0:T(8,128)} %bitcast.11, f32[16,8,128]{2,1,0:T(8,128)} %conc_m.1, ...), custom_call_target="tpu_custom_call" | custom-call | tf_op jit(solution)/shard_map/pallas_call | solution.py:506
  20.7 10.3 %shard_map.96 = (f32[64,8,128]{2,1,0:T(8,128)}, f32[129,8,128]{2,1,0:T(8,128)}) custom-call(s32[56,128]{1,0:T(8,128)} %get-tuple-element.17.pair_list, bf16[64,128,128]{2,1,0:T(8,128)(2,1)} %get-tuple-element.18.x_all, bf16[136,16,128]{2,1,0:T(8,128)(2,1)} %get-tuple-element.19.y_all, f32[64,8,128]{2,1,0:T(8,128)} %bitcast.10, f32[128,8,128]{2,1,0:T(8,128)} %bitcast.8), custom_call_target="tpu_custom_call" | custom-call | tf_op jit(solution)/shard_map/pallas_call | solution.py:529
  31.0 20.3 %shard_map.97 = (f32[16,8,128]{2,1,0:T(8,128)}, f32[16,8,128]{2,1,0:T(8,128)}, f32[4,16,8,128]{3,2,1,0:T(8,128)}, f32[8,16,8,128]{3,2,1,0:T(8,128)}, bf16[64,128,128]{2,1,0:T(8,128)(2,1)}) custom-call(f32[64,8,128]{2,1,0:T(8,128)} %get-tuple-element.22.part_m, f32[129,8,128]{2,1,0:T(8,128)} %get-tuple-element.23.part_i, f32[16,8,128]{2,1,0:T(8,128)} %conc_m.1, ...), custom_call_target="tpu_custom_call" | custom-call | tf_op jit(solution)/shard_map/pallas_call | solution.py:551
  51.4 10.4 %shard_map.98 = (f32[64,8,128]{2,1,0:T(8,128)}, f32[129,8,128]{2,1,0:T(8,128)}) custom-call(s32[56,128]{1,0:T(8,128)} %get-tuple-element.17.pair_list, bf16[64,128,128]{2,1,0:T(8,128)(2,1)} %get-tuple-element.25.x_all, bf16[136,16,128]{2,1,0:T(8,128)(2,1)} %get-tuple-element.19.y_all, f32[64,8,128]{2,1,0:T(8,128)} %bitcast.9, f32[128,8,128]{2,1,0:T(8,128)} %bitcast.7), custom_call_target="tpu_custom_call" | custom-call | tf_op jit(solution)/shard_map/pallas_call | solution.py:529
  61.7 13.8 %shard_map.99 = (f32[16,8,128]{2,1,0:T(8,128)}, f32[16,8,128]{2,1,0:T(8,128)}) custom-call(f32[64,8,128]{2,1,0:T(8,128)} %get-tuple-element.28.part_m, f32[129,8,128]{2,1,0:T(8,128)} %get-tuple-element.29.part_i, f32[16,8,128]{2,1,0:T(8,128)} %get-tuple-element.30.conc_m, f32[16,8,128]{2,1,0:T(8,128)} %get-tuple-element.31.conc_i), custom_call_target="tpu_custom_call" | custom-call | tf_op jit(solution)/shard_map/pallas_call | solution.py:561
  75.5 1.5 %copy.13 = f32[16,8,128]{2,1,0:T(8,128)} copy(f32[16,8,128]{2,1,0:T(8,128)} %get-tuple-element.34) | data formatting | bytes 131072
  77.0 1.5 %copy.14 = f32[16,8,128]{2,1,0:T(8,128)} copy(f32[16,8,128]{2,1,0:T(8,128)} %get-tuple-element.35) | data formatting | bytes 131072
